TPU v7x, 256 devices: a whole 4x4x8 slice. The times are simulated.
256 devices in a mesh: dp: 8 (over x, y_hi), expert: 32 (over z, y_lo, core).
Axes of the slice: x: 4, y: 4 (y_hi: 2, y_lo: 2; y = y_hi * 2 + y_lo), z: 8, core: 2. Of those that a mesh axis runs over, the one named last changes fastest.
Arguments:
- tokens: bfloat16 [3072, 4096], P(('dp', 'expert')), may hold values from -6 to 6
- expert_ids: int32 [3072, 8], P(('dp', 'expert')), may hold values from 0 to 63, all different within a row; in each aligned block of 12 rows (0 to 11, 12 to 23, ...) at most 3 rows name the same one
- gate_probs: float32 [3072, 8], P(('dp', 'expert')), may hold values from 0.02 to 5
- in_weight: bfloat16 [64, 4096, 3072], P('expert', None, 'dp'), may hold values from -0.09375 to 0.09375
- out_weight: bfloat16 [64, 1536, 4096], P('expert', 'dp'), may hold values from -0.15625 to 0.15625
- swap_slot: int32 [32], replicated, may hold values from 0 to 1
Outputs:
- mixed_out: bfloat16 [3072, 4096], P(('dp', 'expert'))
- owner_load: float32 [32], replicated
Inputs may be any that keep to these rules, and one draw needn't show every extreme that they name: `expert_ids`: among the rows of one device no expert is named more than 3 times, and in every draw some device's rows name some expert exactly 3 times; a row names 8 different experts.
All inputs are finite; a program needn't handle non-finite values.
Results may differ from a plain program's by a relative error of at most 0.018.
Values may be sent and summed in bfloat16 or wider, within the bound.
A program may use at most 128 MiB of HBM per device.

v0:
```python
import jax
import jax.numpy as jnp
from jax import lax
from jax.sharding import PartitionSpec as P

BOTH = ("dp", "expert")


def planned_load(mass, swap_slot, per_device, owners, tokens_all):
    experts = jnp.arange(mass.shape[0], dtype=jnp.int32)
    home, within = (experts // per_device, experts % per_device)
    slot = jnp.repeat(swap_slot, per_device)
    holder = jnp.where(within == slot, (home + owners // 2) % owners, home)
    hot = holder[:, None] == jnp.arange(owners, dtype=jnp.int32)
    return jnp.sum(jnp.where(hot, mass[:, None], 0.0), 0) * (owners / tokens_all)


def on_device(tokens, expert_ids, gate_probs, in_weight, out_weight, swap_slot):
    owners = lax.axis_size("expert")
    per_device, width = in_weight.shape[:2]
    half = out_weight.shape[1]
    experts_all = per_device * owners
    experts = jnp.arange(experts_all, dtype=jnp.int32)
    dense = jnp.sum(jnp.where(expert_ids[..., None] == experts, gate_probs[..., None], 0.0), 1)
    all_tokens = lax.all_gather(tokens, BOTH, axis=0, tiled=True)
    all_dense = lax.all_gather(dense, BOTH, axis=0, tiled=True)
    load = planned_load(jnp.sum(all_dense, 0), swap_slot, per_device, owners, all_tokens.shape[0])
    mine = lax.dynamic_slice_in_dim(all_dense, lax.axis_index("expert") * per_device, per_device, 1)
    parts = []
    for s in range(per_device):
        both = jnp.dot(all_tokens, in_weight[s], preferred_element_type=jnp.float32)
        hidden = jax.nn.silu(both[:, :half]) * both[:, half:] * mine[:, s : s + 1]
        parts.append(hidden.astype(jnp.bfloat16))
    mixed = jnp.dot(
        jnp.concatenate(parts, 1),
        out_weight.reshape(per_device * half, width),
        preferred_element_type=jnp.float32,
    ).astype(jnp.bfloat16)
    out = lax.psum_scatter(mixed, BOTH, scatter_dimension=0, tiled=True)
    return (out, load)


def solution(mesh):
    return jax.shard_map(
        on_device,
        mesh=mesh,
        in_specs=(
            P(BOTH, None),
            P(BOTH, None),
            P(BOTH, None),
            P("expert", None, "dp"),
            P("expert", "dp", None),
            P(),
        ),
        out_specs=(P(BOTH, None), P()),
        check_vma=False,
    )
```

profile of v0, /device:TPU:6, one launch (start us, length us, event | category | flops | bytes accessed | tf_op | source)
XLA Modules:
  0.0 2044.4 jit_solution(17175509425682315164)
XLA Ops:
  9.8 336.8 %all-gather.1 = f32[256,12,64]{2,1,0:T(8,128)} all-gather(f32[1,12,64]{2,1,0:T(8,128)S(1)} %bitcast.14), channel_id=1, replica_groups=mesh['dp'=8,'expert'=32] {'dp','expert'}, dimensions={0}, use_global_device_ids=true | all-gather | bytes 789504 | tf_op jit(solution)/shard_map/all_gather | solution.py:26
  352.7 104.2 %all-gather.4.cloned.1.call-done = bf16[256,12,4096]{2,1,0:T(8,128)(2,1)} async-done(((bf16[1,12,4096]{2,1,0:T(8,128)(2,1)}), bf16[256,12,4096]{2,1,0:T(8,128)(2,1)}) %all-gather.4.cloned.1.call-update) | async-done | bytes 25165840 | tf_op jit(solution)/shard_map/all_gather | solution.py:25
  457.0 34.8 %reshape.54 = bf16[3072,4096]{1,0:T(8,128)(2,1)} reshape(bf16[256,12,4096]{2,1,0:T(8,128)(2,1)} %all-gather.4.cloned.1.call-done) | data formatting | bytes 50331648
  491.8 14.5 fusion.1
  506.3 16.3 fusion.3
  526.8 18.4 convolution_convert_fusion
  545.3 661.3 %fusion = bf16[16,4096]{1,0:T(8,128)(2,1)S(1)} fusion(bf16[3072,4096]{1,0:T(8,128)(2,1)} %convolution_convert_fusion), kind=kCustom, calls=%all-reduce-scatter | all-reduce-scatter fusion | flops 16777216 | bytes 25296896
  1206.6 77.1 %collective-permute-start.62 = (bf16[16,4096]{1,0:T(8,128)(2,1)S(1)}, bf16[16,4096]{1,0:T(8,128)(2,1)S(1)}, u32[]{:S(2)}, u32[]{:S(2)}) collective-permute-start(bf16[16,4096]{1,0:T(8,128)(2,1)S(1)} %fusion), channel_id=1, source_target_pairs={{0,63},{1,64},{2,65},{3,66},{4,67},{5,68},{6,69},{7,70},{8,71},{9,... | collective-permute-start | bytes 393224
  1311.1 25.9 %collective-permute-done.57 = bf16[16,4096]{1,0:T(8,128)(2,1)S(1)} collective-permute-done((bf16[16,4096]{1,0:T(8,128)(2,1)S(1)}, bf16[16,4096]{1,0:T(8,128)(2,1)S(1)}, u32[]{:S(2)}, u32[]{:S(2)}) %collective-permute-start.57) | collective-permute-done | bytes 131104
  1338.9 16.6 collective-permute-done.56
  1392.9 16.0 collective-permute-done.45
  1468.1 22.1 %collective-permute-start.28 = (bf16[16,4096]{1,0:T(8,128)(2,1)S(1)}, bf16[16,4096]{1,0:T(8,128)(2,1)S(1)}, u32[]{:S(2)}, u32[]{:S(2)}) collective-permute-start(bf16[16,4096]{1,0:T(8,128)(2,1)S(1)} %fusion), channel_id=1, source_target_pairs={{0,29},{1,30},{2,31},{3,32},{4,33},{5,34},{6,35},{7,36},{8,37},{9,... | collective-permute-start | bytes 393224
  1490.2 13.1 collective-permute-start.27
  1556.0 13.1 collective-permute-start.22
  1569.1 13.1 collective-permute-start.21
  1582.3 13.1 collective-permute-start.20
  1595.4 13.1 collective-permute-start.19
  1608.6 13.1 collective-permute-start.18
  1621.7 13.1 collective-permute-start.17
  1634.9 13.1 collective-permute-start.16
  1648.0 13.1 collective-permute-start.15
  1661.2 13.1 collective-permute-start.14
  1674.3 13.1 collective-permute-start.13
  1687.4 13.1 collective-permute-start.12
  1700.6 13.1 collective-permute-start.11
  1714.1 13.1 collective-permute-start.10
  1741.7 13.1 collective-permute-start.8
  1754.9 13.1 collective-permute-start.7
  1768.0 13.1 collective-permute-start.6
  1781.1 13.1 collective-permute-start.5
  1849.8 13.1 collective-permute-start
  1872.4 163.5 %concatenate.4 = bf16[1036,4096]{1,0:T(8,128)(2,1)} concatenate(bf16[12,4096]{1,0:T(8,128)(2,1)} %copy-done.2, bf16[16,4096]{1,0:T(8,128)(2,1)S(1)} %collective-permute-done.62, bf16[16,4096]{1,0:T(8,128)(2,1)S(1)} %collective-permute-done.61, bf16[16,4096]{1,0:T(8,128)(2,1)} %copy-done.1, bf16[16,4096]{1,0:T(8,128)(2,1)} %copy-done.3, bf16[16,4096]{1,0:T(8,128)(2,1)} %copy-done.4, ...), dimensions={0} | concatenate | bytes 16973824
  (208 shorter events, 272.0 us)
Async XLA Ops:
  7.2 449.8 %all-gather.4.cloned.1.call-start = ((), (), s32[]{:S(2)}) async-start(), calls=%async_computation | async-start | bytes 33685504 | tf_op jit(solution)/shard_map/all_gather | solution.py:25
  1206.6 93.4 %collective-permute-start.62 = (bf16[16,4096]{1,0:T(8,128)(2,1)S(1)}, bf16[16,4096]{1,0:T(8,128)(2,1)S(1)}, u32[]{:S(2)}, u32[]{:S(2)}) collective-permute-start(bf16[16,4096]{1,0:T(8,128)(2,1)S(1)} %fusion), channel_id=1, source_target_pairs={{0,63},{1,64},{2,65},{3,66},{4,67},{5,68},{6,69},{7,70},{8,71},{9,... | collective-permute-start | bytes 393224
  1303.9 54.5 %collective-permute-start.55 = (bf16[16,4096]{1,0:T(8,128)(2,1)S(1)}, bf16[16,4096]{1,0:T(8,128)(2,1)S(1)}, u32[]{:S(2)}, u32[]{:S(2)}) collective-permute-start(bf16[16,4096]{1,0:T(8,128)(2,1)S(1)} %fusion), channel_id=1, source_target_pairs={{0,56},{1,57},{2,58},{3,59},{4,60},{5,61},{6,62},{7,63},{8,64},{9,... | collective-permute-start | bytes 393224
  1305.9 55.3 %collective-permute-start.54 = (bf16[16,4096]{1,0:T(8,128)(2,1)S(1)}, bf16[16,4096]{1,0:T(8,128)(2,1)S(1)}, u32[]{:S(2)}, u32[]{:S(2)}) collective-permute-start(bf16[16,4096]{1,0:T(8,128)(2,1)S(1)} %fusion), channel_id=1, source_target_pairs={{0,55},{1,56},{2,57},{3,58},{4,59},{5,60},{6,61},{7,62},{8,63},{9,... | collective-permute-start | bytes 393224
  1309.2 54.8 %collective-permute-start.53 = (bf16[16,4096]{1,0:T(8,128)(2,1)S(1)}, bf16[16,4096]{1,0:T(8,128)(2,1)S(1)}, u32[]{:S(2)}, u32[]{:S(2)}) collective-permute-start(bf16[16,4096]{1,0:T(8,128)(2,1)S(1)} %fusion), channel_id=1, source_target_pairs={{0,54},{1,55},{2,56},{3,57},{4,58},{5,59},{6,60},{7,61},{8,62},{9,... | collective-permute-start | bytes 393224
  1458.6 57.9 %collective-permute-start.30 = (bf16[16,4096]{1,0:T(8,128)(2,1)S(1)}, bf16[16,4096]{1,0:T(8,128)(2,1)S(1)}, u32[]{:S(2)}, u32[]{:S(2)}) collective-permute-start(bf16[16,4096]{1,0:T(8,128)(2,1)S(1)} %fusion), channel_id=1, source_target_pairs={{0,31},{1,32},{2,33},{3,34},{4,35},{5,36},{6,37},{7,38},{8,39},{9,... | collective-permute-start | bytes 393224
  1460.5 69.1 %collective-permute-start.29 = (bf16[16,4096]{1,0:T(8,128)(2,1)S(1)}, bf16[16,4096]{1,0:T(8,128)(2,1)S(1)}, u32[]{:S(2)}, u32[]{:S(2)}) collective-permute-start(bf16[16,4096]{1,0:T(8,128)(2,1)S(1)} %fusion), channel_id=1, source_target_pairs={{0,30},{1,31},{2,32},{3,33},{4,34},{5,35},{6,36},{7,37},{8,38},{9,... | collective-permute-start | bytes 393224
  1468.1 74.7 %collective-permute-start.28 = (bf16[16,4096]{1,0:T(8,128)(2,1)S(1)}, bf16[16,4096]{1,0:T(8,128)(2,1)S(1)}, u32[]{:S(2)}, u32[]{:S(2)}) collective-permute-start(bf16[16,4096]{1,0:T(8,128)(2,1)S(1)} %fusion), channel_id=1, source_target_pairs={{0,29},{1,30},{2,31},{3,32},{4,33},{5,34},{6,35},{7,36},{8,37},{9,... | collective-permute-start | bytes 393224
  1490.2 65.7 %collective-permute-start.27 = (bf16[16,4096]{1,0:T(8,128)(2,1)S(1)}, bf16[16,4096]{1,0:T(8,128)(2,1)S(1)}, u32[]{:S(2)}, u32[]{:S(2)}) collective-permute-start(bf16[16,4096]{1,0:T(8,128)(2,1)S(1)} %fusion), channel_id=1, source_target_pairs={{0,28},{1,29},{2,30},{3,31},{4,32},{5,33},{6,34},{7,35},{8,36},{9,... | collective-permute-start | bytes 393224
  1503.4 65.7 %collective-permute-start.26 = (bf16[16,4096]{1,0:T(8,128)(2,1)S(1)}, bf16[16,4096]{1,0:T(8,128)(2,1)S(1)}, u32[]{:S(2)}, u32[]{:S(2)}) collective-permute-start(bf16[16,4096]{1,0:T(8,128)(2,1)S(1)} %fusion), channel_id=1, source_target_pairs={{0,27},{1,28},{2,29},{3,30},{4,31},{5,32},{6,33},{7,34},{8,35},{9,... | collective-permute-start | bytes 393224
  1516.5 65.7 %collective-permute-start.25 = (bf16[16,4096]{1,0:T(8,128)(2,1)S(1)}, bf16[16,4096]{1,0:T(8,128)(2,1)S(1)}, u32[]{:S(2)}, u32[]{:S(2)}) collective-permute-start(bf16[16,4096]{1,0:T(8,128)(2,1)S(1)} %fusion), channel_id=1, source_target_pairs={{0,26},{1,27},{2,28},{3,29},{4,30},{5,31},{6,32},{7,33},{8,34},{9,... | collective-permute-start | bytes 393224
  1529.7 65.7 %collective-permute-start.24 = (bf16[16,4096]{1,0:T(8,128)(2,1)S(1)}, bf16[16,4096]{1,0:T(8,128)(2,1)S(1)}, u32[]{:S(2)}, u32[]{:S(2)}) collective-permute-start(bf16[16,4096]{1,0:T(8,128)(2,1)S(1)} %fusion), channel_id=1, source_target_pairs={{0,25},{1,26},{2,27},{3,28},{4,29},{5,30},{6,31},{7,32},{8,33},{9,... | collective-permute-start | bytes 393224
  1542.8 65.7 %collective-permute-start.23 = (bf16[16,4096]{1,0:T(8,128)(2,1)S(1)}, bf16[16,4096]{1,0:T(8,128)(2,1)S(1)}, u32[]{:S(2)}, u32[]{:S(2)}) collective-permute-start(bf16[16,4096]{1,0:T(8,128)(2,1)S(1)} %fusion), channel_id=1, source_target_pairs={{0,24},{1,25},{2,26},{3,27},{4,28},{5,29},{6,30},{7,31},{8,32},{9,... | collective-permute-start | bytes 393224
  1556.0 65.7 %collective-permute-start.22 = (bf16[16,4096]{1,0:T(8,128)(2,1)S(1)}, bf16[16,4096]{1,0:T(8,128)(2,1)}, u32[]{:S(2)}, u32[]{:S(2)}) collective-permute-start(bf16[16,4096]{1,0:T(8,128)(2,1)S(1)} %fusion), channel_id=1, source_target_pairs={{0,23},{1,24},{2,25},{3,26},{4,27},{5,28},{6,29},{7,30},{8,31},{9,... | collective-permute-start | bytes 393224
  1569.1 65.7 %collective-permute-start.21 = (bf16[16,4096]{1,0:T(8,128)(2,1)S(1)}, bf16[16,4096]{1,0:T(8,128)(2,1)}, u32[]{:S(2)}, u32[]{:S(2)}) collective-permute-start(bf16[16,4096]{1,0:T(8,128)(2,1)S(1)} %fusion), channel_id=1, source_target_pairs={{0,22},{1,23},{2,24},{3,25},{4,26},{5,27},{6,28},{7,29},{8,30},{9,... | collective-permute-start | bytes 393224
  1582.3 65.7 %collective-permute-start.20 = (bf16[16,4096]{1,0:T(8,128)(2,1)S(1)}, bf16[16,4096]{1,0:T(8,128)(2,1)}, u32[]{:S(2)}, u32[]{:S(2)}) collective-permute-start(bf16[16,4096]{1,0:T(8,128)(2,1)S(1)} %fusion), channel_id=1, source_target_pairs={{0,21},{1,22},{2,23},{3,24},{4,25},{5,26},{6,27},{7,28},{8,29},{9,... | collective-permute-start | bytes 393224
  1595.4 65.7 %collective-permute-start.19 = (bf16[16,4096]{1,0:T(8,128)(2,1)S(1)}, bf16[16,4096]{1,0:T(8,128)(2,1)}, u32[]{:S(2)}, u32[]{:S(2)}) collective-permute-start(bf16[16,4096]{1,0:T(8,128)(2,1)S(1)} %fusion), channel_id=1, source_target_pairs={{0,20},{1,21},{2,22},{3,23},{4,24},{5,25},{6,26},{7,27},{8,28},{9,... | collective-permute-start | bytes 393224
  1608.6 65.7 %collective-permute-start.18 = (bf16[16,4096]{1,0:T(8,128)(2,1)S(1)}, bf16[16,4096]{1,0:T(8,128)(2,1)}, u32[]{:S(2)}, u32[]{:S(2)}) collective-permute-start(bf16[16,4096]{1,0:T(8,128)(2,1)S(1)} %fusion), channel_id=1, source_target_pairs={{0,19},{1,20},{2,21},{3,22},{4,23},{5,24},{6,25},{7,26},{8,27},{9,... | collective-permute-start | bytes 393224
  1621.7 65.7 %collective-permute-start.17 = (bf16[16,4096]{1,0:T(8,128)(2,1)S(1)}, bf16[16,4096]{1,0:T(8,128)(2,1)}, u32[]{:S(2)}, u32[]{:S(2)}) collective-permute-start(bf16[16,4096]{1,0:T(8,128)(2,1)S(1)} %fusion), channel_id=1, source_target_pairs={{0,18},{1,19},{2,20},{3,21},{4,22},{5,23},{6,24},{7,25},{8,26},{9,... | collective-permute-start | bytes 393224
  1634.9 65.7 %collective-permute-start.16 = (bf16[16,4096]{1,0:T(8,128)(2,1)S(1)}, bf16[16,4096]{1,0:T(8,128)(2,1)}, u32[]{:S(2)}, u32[]{:S(2)}) collective-permute-start(bf16[16,4096]{1,0:T(8,128)(2,1)S(1)} %fusion), channel_id=1, source_target_pairs={{0,17},{1,18},{2,19},{3,20},{4,21},{5,22},{6,23},{7,24},{8,25},{9,... | collective-permute-start | bytes 393224
  1648.0 65.7 %collective-permute-start.15 = (bf16[16,4096]{1,0:T(8,128)(2,1)S(1)}, bf16[16,4096]{1,0:T(8,128)(2,1)}, u32[]{:S(2)}, u32[]{:S(2)}) collective-permute-start(bf16[16,4096]{1,0:T(8,128)(2,1)S(1)} %fusion), channel_id=1, source_target_pairs={{0,16},{1,17},{2,18},{3,19},{4,20},{5,21},{6,22},{7,23},{8,24},{9,... | collective-permute-start | bytes 393224
  1661.2 67.4 %collective-permute-start.14 = (bf16[16,4096]{1,0:T(8,128)(2,1)S(1)}, bf16[16,4096]{1,0:T(8,128)(2,1)}, u32[]{:S(2)}, u32[]{:S(2)}) collective-permute-start(bf16[16,4096]{1,0:T(8,128)(2,1)S(1)} %fusion), channel_id=1, source_target_pairs={{0,15},{1,16},{2,17},{3,18},{4,19},{5,20},{6,21},{7,22},{8,23},{9,... | collective-permute-start | bytes 393224
  1674.3 67.4 %collective-permute-start.13 = (bf16[16,4096]{1,0:T(8,128)(2,1)S(1)}, bf16[16,4096]{1,0:T(8,128)(2,1)}, u32[]{:S(2)}, u32[]{:S(2)}) collective-permute-start(bf16[16,4096]{1,0:T(8,128)(2,1)S(1)} %fusion), channel_id=1, source_target_pairs={{0,14},{1,15},{2,16},{3,17},{4,18},{5,19},{6,20},{7,21},{8,22},{9,... | collective-permute-start | bytes 393224
  1687.4 67.4 %collective-permute-start.12 = (bf16[16,4096]{1,0:T(8,128)(2,1)S(1)}, bf16[16,4096]{1,0:T(8,128)(2,1)}, u32[]{:S(2)}, u32[]{:S(2)}) collective-permute-start(bf16[16,4096]{1,0:T(8,128)(2,1)S(1)} %fusion), channel_id=1, source_target_pairs={{0,13},{1,14},{2,15},{3,16},{4,17},{5,18},{6,19},{7,20},{8,21},{9,... | collective-permute-start | bytes 393224
  1700.6 67.4 %collective-permute-start.11 = (bf16[16,4096]{1,0:T(8,128)(2,1)S(1)}, bf16[16,4096]{1,0:T(8,128)(2,1)}, u32[]{:S(2)}, u32[]{:S(2)}) collective-permute-start(bf16[16,4096]{1,0:T(8,128)(2,1)S(1)} %fusion), channel_id=1, source_target_pairs={{0,12},{1,13},{2,14},{3,15},{4,16},{5,17},{6,18},{7,19},{8,20},{9,... | collective-permute-start | bytes 393224
  1714.1 67.0 %collective-permute-start.10 = (bf16[16,4096]{1,0:T(8,128)(2,1)S(1)}, bf16[16,4096]{1,0:T(8,128)(2,1)}, u32[]{:S(2)}, u32[]{:S(2)}) collective-permute-start(bf16[16,4096]{1,0:T(8,128)(2,1)S(1)} %fusion), channel_id=1, source_target_pairs={{0,11},{1,12},{2,13},{3,14},{4,15},{5,16},{6,17},{7,18},{8,19},{9,... | collective-permute-start | bytes 393224
  1728.6 68.6 %collective-permute-start.9 = (bf16[16,4096]{1,0:T(8,128)(2,1)S(1)}, bf16[16,4096]{1,0:T(8,128)(2,1)}, u32[]{:S(2)}, u32[]{:S(2)}) collective-permute-start(bf16[16,4096]{1,0:T(8,128)(2,1)S(1)} %fusion), channel_id=1, source_target_pairs={{0,10},{1,11},{2,12},{3,13},{4,14},{5,15},{6,16},{7,17},{8,18},{9,... | collective-permute-start | bytes 393224
  1741.7 68.6 %collective-permute-start.8 = (bf16[16,4096]{1,0:T(8,128)(2,1)S(1)}, bf16[16,4096]{1,0:T(8,128)(2,1)}, u32[]{:S(2)}, u32[]{:S(2)}) collective-permute-start(bf16[16,4096]{1,0:T(8,128)(2,1)S(1)} %fusion), channel_id=1, source_target_pairs={{0,9},{1,10},{2,11},{3,12},{4,13},{5,14},{6,15},{7,16},{8,17},{9,1... | collective-permute-start | bytes 393224
  1754.9 68.6 %collective-permute-start.7 = (bf16[16,4096]{1,0:T(8,128)(2,1)S(1)}, bf16[16,4096]{1,0:T(8,128)(2,1)}, u32[]{:S(2)}, u32[]{:S(2)}) collective-permute-start(bf16[16,4096]{1,0:T(8,128)(2,1)S(1)} %fusion), channel_id=1, source_target_pairs={{0,8},{1,9},{2,10},{3,11},{4,12},{5,13},{6,14},{7,15},{8,16},{9,17... | collective-permute-start | bytes 393224
  1768.0 68.6 %collective-permute-start.6 = (bf16[16,4096]{1,0:T(8,128)(2,1)S(1)}, bf16[16,4096]{1,0:T(8,128)(2,1)}, u32[]{:S(2)}, u32[]{:S(2)}) collective-permute-start(bf16[16,4096]{1,0:T(8,128)(2,1)S(1)} %fusion), channel_id=1, source_target_pairs={{0,7},{1,8},{2,9},{3,10},{4,11},{5,12},{6,13},{7,14},{8,15},{9,16}... | collective-permute-start | bytes 393224
  1781.1 68.6 %collective-permute-start.5 = (bf16[16,4096]{1,0:T(8,128)(2,1)S(1)}, bf16[16,4096]{1,0:T(8,128)(2,1)}, u32[]{:S(2)}, u32[]{:S(2)}) collective-permute-start(bf16[16,4096]{1,0:T(8,128)(2,1)S(1)} %fusion), channel_id=1, source_target_pairs={{0,6},{1,7},{2,8},{3,9},{4,10},{5,11},{6,12},{7,13},{8,14},{9,15},... | collective-permute-start | bytes 393224
  1797.2 66.2 %collective-permute-start.4 = (bf16[16,4096]{1,0:T(8,128)(2,1)S(1)}, bf16[16,4096]{1,0:T(8,128)(2,1)S(1)}, u32[]{:S(2)}, u32[]{:S(2)}) collective-permute-start(bf16[16,4096]{1,0:T(8,128)(2,1)S(1)} %fusion), channel_id=1, source_target_pairs={{0,5},{1,6},{2,7},{3,8},{4,9},{5,10},{6,11},{7,12},{8,13},{9,14},{... | collective-permute-start | bytes 393224
  (77 other events, 12414.3 us)
Sparse Core Ops, SparseCore 0:
  9.9 447.0 all-gather.3
where the time goes:
time: 2050 us; the launch traced here: 2040 us
  blocking collectives  998 us (49%)
  starting transfers between devices  531 us (26%)
  waiting for transfers between devices  232 us (11%)
  local copies, waits for them, and re-layouts  211 us (10%)
  matrix products  49.2 us (2%)
    unnamed x1, blocking collectives  661 us
    unnamed x64, starting transfers between devices  531 us
    all_gather x1, blocking collectives, on_device(): all_dense = lax.all_gather(dense, BOTH, axis=0, tiled=True)  337 us
    unnamed x95, local copies, waits for them, and re-layouts  206 us
    unnamed x65, waiting for transfers between devices  128 us
    all_gather x1, waiting for transfers between devices, on_device(): all_tokens = lax.all_gather(tokens, BOTH, axis=0, tiled=True)  104 us
  transfers between devices with their start and end apart: 65, of which 22 were waited for; matrix products, arithmetic and copies ran while one was open for 1% of the time, Pallas kernels for 0%

commit v1 on v0

--- a/solution.py
+++ b/solution.py
@@ -23,7 +23,9 @@
     experts = jnp.arange(experts_all, dtype=jnp.int32)
     dense = jnp.sum(jnp.where(expert_ids[..., None] == experts, gate_probs[..., None], 0.0), 1)
     all_tokens = lax.all_gather(tokens, BOTH, axis=0, tiled=True)
-    all_dense = lax.all_gather(dense, BOTH, axis=0, tiled=True)
+    all_dense = jnp.concatenate(
+        lax.all_to_all(jnp.stack([dense] * lax.axis_size(BOTH)), BOTH, 0, 0), axis=0
+    )
     load = planned_load(jnp.sum(all_dense, 0), swap_slot, per_device, owners, all_tokens.shape[0])
     mine = lax.dynamic_slice_in_dim(all_dense, lax.axis_index("expert") * per_device, per_device, 1)
     parts = []

time: 2050 us -> 2060 us (level)
  blocking collectives: 998 us -> 662 us
  waiting for transfers between devices: 232 us -> 553 us
    all_gather x1 -> x0, blocking collectives: 337 us -> none  [on_device(): all_dense = lax.all_gather(dense, BOTH, axis=0, tiled=True)]
    all_gather x1, waiting for transfers between devices: 104 us -> 395 us  [on_device(): all_tokens = lax.all_gather(tokens, BOTH, axis=0, tiled=True)]
    all_to_all x0 -> x1, waiting for transfers between devices: none -> 28.2 us  [on_device(): lax.all_to_all(jnp.stack([dense] * lax.axis_size(BOTH)), BOTH, 0, 0)]
    unnamed x95 -> x96, local copies, waits for them, and re-layouts: 206 us -> 210 us
  transfers between devices with their start and end apart: 65 -> 66, of which waited for: 22 -> 23; matrix products, arithmetic and copies ran while one was open for 1% -> 1% of each run, Pallas kernels for 0% -> 0%
where the time goes in v1:
time: 2060 us; the launch traced here: 2050 us
  blocking collectives  662 us (32%)
  waiting for transfers between devices  553 us (27%)
  starting transfers between devices  536 us (26%)
  local copies, waits for them, and re-layouts  219 us (11%)
  matrix products  49.3 us (2%)
    unnamed x1, blocking collectives  662 us
    unnamed x64, starting transfers between devices  521 us
    all_gather x1, waiting for transfers between devices, on_device(): all_tokens = lax.all_gather(tokens, BOTH, axis=0, tiled=True)  395 us
    unnamed x96, local copies, waits for them, and re-layouts  210 us
    unnamed x65, waiting for transfers between devices  129 us
  transfers between devices with their start and end apart: 66, of which 23 were waited for; matrix products, arithmetic and copies ran while one was open for 1% of the time, Pallas kernels for 0%

profile of v1, /device:TPU:6, one launch (start us, length us, event | category | flops | bytes accessed | tf_op | source)
XLA Modules:
  0.0 2047.1 jit_solution(14832558013695053929)
XLA Ops:
  14.4 15.5 all-to-all-start
  29.9 28.2 %all-to-all-done = f32[256,1,768]{2,1,0:T(1,128)} async-done(((f32[256,1,768]{2,1,0:T(1,128)}), f32[256,1,768]{2,1,0:T(1,128)}, u32[]{:S(2)}, u32[]{:S(2)}) %all-to-all-start) | async-done | bytes 786464 | tf_op jit(solution)/shard_map/all_to_all | solution.py:27
  72.0 395.4 %all-gather.3.cloned.1.call-done = bf16[256,12,4096]{2,1,0:T(8,128)(2,1)} async-done(((bf16[1,12,4096]{2,1,0:T(8,128)(2,1)}), bf16[256,12,4096]{2,1,0:T(8,128)(2,1)}) %all-gather.3.cloned.1.call-update) | async-done | bytes 25165840 | tf_op jit(solution)/shard_map/all_gather | solution.py:25
  467.4 34.8 %reshape.60 = bf16[3072,4096]{1,0:T(8,128)(2,1)} reshape(bf16[256,12,4096]{2,1,0:T(8,128)(2,1)} %all-gather.3.cloned.1.call-done) | data formatting | bytes 50331648
  502.2 14.5 fusion.1
  516.8 16.4 fusion.3
  537.4 18.5 convolution_convert_fusion
  555.9 661.7 %fusion = bf16[16,4096]{1,0:T(8,128)(2,1)S(1)} fusion(bf16[3072,4096]{1,0:T(8,128)(2,1)} %convolution_convert_fusion), kind=kCustom, calls=%all-reduce-scatter | all-reduce-scatter fusion | flops 16777216 | bytes 25296896
  1217.6 77.1 %collective-permute-start.62 = (bf16[16,4096]{1,0:T(8,128)(2,1)S(1)}, bf16[16,4096]{1,0:T(8,128)(2,1)S(1)}, u32[]{:S(2)}, u32[]{:S(2)}) collective-permute-start(bf16[16,4096]{1,0:T(8,128)(2,1)S(1)} %fusion), channel_id=1, source_target_pairs={{0,63},{1,64},{2,65},{3,66},{4,67},{5,68},{6,69},{7,70},{8,71},{9,... | collective-permute-start | bytes 393224
  1322.1 25.9 %collective-permute-done.57 = bf16[16,4096]{1,0:T(8,128)(2,1)S(1)} collective-permute-done((bf16[16,4096]{1,0:T(8,128)(2,1)S(1)}, bf16[16,4096]{1,0:T(8,128)(2,1)S(1)}, u32[]{:S(2)}, u32[]{:S(2)}) %collective-permute-start.57) | collective-permute-done | bytes 131104
  1349.9 16.6 collective-permute-done.56
  1403.9 16.0 collective-permute-done.45
  1482.4 23.0 %collective-permute-start.27 = (bf16[16,4096]{1,0:T(8,128)(2,1)S(1)}, bf16[16,4096]{1,0:T(8,128)(2,1)S(1)}, u32[]{:S(2)}, u32[]{:S(2)}) collective-permute-start(bf16[16,4096]{1,0:T(8,128)(2,1)S(1)} %fusion), channel_id=1, source_target_pairs={{0,28},{1,29},{2,30},{3,31},{4,32},{5,33},{6,34},{7,35},{8,36},{9,... | collective-permute-start | bytes 393224
  1558.0 13.1 collective-permute-start.22
  1571.2 13.1 collective-permute-start.21
  1584.3 13.1 collective-permute-start.20
  1597.5 13.1 collective-permute-start.19
  1610.7 13.1 collective-permute-start.18
  1623.8 13.1 collective-permute-start.17
  1636.9 13.1 collective-permute-start.16
  1650.1 13.1 collective-permute-start.15
  1663.2 13.1 collective-permute-start.14
  1676.4 13.1 collective-permute-start.13
  1689.5 13.1 collective-permute-start.12
  1702.6 13.1 collective-permute-start.11
  1716.2 13.1 collective-permute-start.10
  1743.8 13.1 collective-permute-start.8
  1756.9 13.1 collective-permute-start.7
  1770.1 13.1 collective-permute-start.6
  1783.2 13.1 collective-permute-start.5
  1851.8 13.1 collective-permute-start
  1874.5 164.2 %concatenate.4 = bf16[1036,4096]{1,0:T(8,128)(2,1)} concatenate(bf16[12,4096]{1,0:T(8,128)(2,1)} %copy-done.2, bf16[16,4096]{1,0:T(8,128)(2,1)S(1)} %collective-permute-done.62, bf16[16,4096]{1,0:T(8,128)(2,1)S(1)} %collective-permute-done.61, bf16[16,4096]{1,0:T(8,128)(2,1)} %copy-done.1, bf16[16,4096]{1,0:T(8,128)(2,1)} %copy-done.3, bf16[16,4096]{1,0:T(8,128)(2,1)} %copy-done.4, ...), dimensions={0} | concatenate | bytes 16973824
  (214 shorter events, 287.7 us)
Async XLA Ops:
  7.2 460.3 %all-gather.3.cloned.1.call-start = ((), (), s32[]{:S(2)}) async-start(), calls=%async_computation.1 | async-start | bytes 33685504 | tf_op jit(solution)/shard_map/all_gather | solution.py:25
  1217.6 93.4 %collective-permute-start.62 = (bf16[16,4096]{1,0:T(8,128)(2,1)S(1)}, bf16[16,4096]{1,0:T(8,128)(2,1)S(1)}, u32[]{:S(2)}, u32[]{:S(2)}) collective-permute-start(bf16[16,4096]{1,0:T(8,128)(2,1)S(1)} %fusion), channel_id=1, source_target_pairs={{0,63},{1,64},{2,65},{3,66},{4,67},{5,68},{6,69},{7,70},{8,71},{9,... | collective-permute-start | bytes 393224
  1313.0 53.6 %collective-permute-start.56 = (bf16[16,4096]{1,0:T(8,128)(2,1)S(1)}, bf16[16,4096]{1,0:T(8,128)(2,1)S(1)}, u32[]{:S(2)}, u32[]{:S(2)}) collective-permute-start(bf16[16,4096]{1,0:T(8,128)(2,1)S(1)} %fusion), channel_id=1, source_target_pairs={{0,57},{1,58},{2,59},{3,60},{4,61},{5,62},{6,63},{7,64},{8,65},{9,... | collective-permute-start | bytes 393224
  1314.9 54.5 %collective-permute-start.55 = (bf16[16,4096]{1,0:T(8,128)(2,1)S(1)}, bf16[16,4096]{1,0:T(8,128)(2,1)S(1)}, u32[]{:S(2)}, u32[]{:S(2)}) collective-permute-start(bf16[16,4096]{1,0:T(8,128)(2,1)S(1)} %fusion), channel_id=1, source_target_pairs={{0,56},{1,57},{2,58},{3,59},{4,60},{5,61},{6,62},{7,63},{8,64},{9,... | collective-permute-start | bytes 393224
  1316.9 55.3 %collective-permute-start.54 = (bf16[16,4096]{1,0:T(8,128)(2,1)S(1)}, bf16[16,4096]{1,0:T(8,128)(2,1)S(1)}, u32[]{:S(2)}, u32[]{:S(2)}) collective-permute-start(bf16[16,4096]{1,0:T(8,128)(2,1)S(1)} %fusion), channel_id=1, source_target_pairs={{0,55},{1,56},{2,57},{3,58},{4,59},{5,60},{6,61},{7,62},{8,63},{9,... | collective-permute-start | bytes 393224
  1320.2 54.8 %collective-permute-start.53 = (bf16[16,4096]{1,0:T(8,128)(2,1)S(1)}, bf16[16,4096]{1,0:T(8,128)(2,1)S(1)}, u32[]{:S(2)}, u32[]{:S(2)}) collective-permute-start(bf16[16,4096]{1,0:T(8,128)(2,1)S(1)} %fusion), channel_id=1, source_target_pairs={{0,54},{1,55},{2,56},{3,57},{4,58},{5,59},{6,60},{7,61},{8,62},{9,... | collective-permute-start | bytes 393224
  1471.5 60.2 %collective-permute-start.29 = (bf16[16,4096]{1,0:T(8,128)(2,1)S(1)}, bf16[16,4096]{1,0:T(8,128)(2,1)S(1)}, u32[]{:S(2)}, u32[]{:S(2)}) collective-permute-start(bf16[16,4096]{1,0:T(8,128)(2,1)S(1)} %fusion), channel_id=1, source_target_pairs={{0,30},{1,31},{2,32},{3,33},{4,34},{5,35},{6,36},{7,37},{8,38},{9,... | collective-permute-start | bytes 393224
  1480.5 64.4 %collective-permute-start.28 = (bf16[16,4096]{1,0:T(8,128)(2,1)S(1)}, bf16[16,4096]{1,0:T(8,128)(2,1)S(1)}, u32[]{:S(2)}, u32[]{:S(2)}) collective-permute-start(bf16[16,4096]{1,0:T(8,128)(2,1)S(1)} %fusion), channel_id=1, source_target_pairs={{0,29},{1,30},{2,31},{3,32},{4,33},{5,34},{6,35},{7,36},{8,37},{9,... | collective-permute-start | bytes 393224
  1482.4 75.6 %collective-permute-start.27 = (bf16[16,4096]{1,0:T(8,128)(2,1)S(1)}, bf16[16,4096]{1,0:T(8,128)(2,1)S(1)}, u32[]{:S(2)}, u32[]{:S(2)}) collective-permute-start(bf16[16,4096]{1,0:T(8,128)(2,1)S(1)} %fusion), channel_id=1, source_target_pairs={{0,28},{1,29},{2,30},{3,31},{4,32},{5,33},{6,34},{7,35},{8,36},{9,... | collective-permute-start | bytes 393224
  1505.4 65.7 %collective-permute-start.26 = (bf16[16,4096]{1,0:T(8,128)(2,1)S(1)}, bf16[16,4096]{1,0:T(8,128)(2,1)S(1)}, u32[]{:S(2)}, u32[]{:S(2)}) collective-permute-start(bf16[16,4096]{1,0:T(8,128)(2,1)S(1)} %fusion), channel_id=1, source_target_pairs={{0,27},{1,28},{2,29},{3,30},{4,31},{5,32},{6,33},{7,34},{8,35},{9,... | collective-permute-start | bytes 393224
  1518.6 65.7 %collective-permute-start.25 = (bf16[16,4096]{1,0:T(8,128)(2,1)S(1)}, bf16[16,4096]{1,0:T(8,128)(2,1)S(1)}, u32[]{:S(2)}, u32[]{:S(2)}) collective-permute-start(bf16[16,4096]{1,0:T(8,128)(2,1)S(1)} %fusion), channel_id=1, source_target_pairs={{0,26},{1,27},{2,28},{3,29},{4,30},{5,31},{6,32},{7,33},{8,34},{9,... | collective-permute-start | bytes 393224
  1531.7 65.7 %collective-permute-start.24 = (bf16[16,4096]{1,0:T(8,128)(2,1)S(1)}, bf16[16,4096]{1,0:T(8,128)(2,1)S(1)}, u32[]{:S(2)}, u32[]{:S(2)}) collective-permute-start(bf16[16,4096]{1,0:T(8,128)(2,1)S(1)} %fusion), channel_id=1, source_target_pairs={{0,25},{1,26},{2,27},{3,28},{4,29},{5,30},{6,31},{7,32},{8,33},{9,... | collective-permute-start | bytes 393224
  1544.9 65.7 %collective-permute-start.23 = (bf16[16,4096]{1,0:T(8,128)(2,1)S(1)}, bf16[16,4096]{1,0:T(8,128)(2,1)S(1)}, u32[]{:S(2)}, u32[]{:S(2)}) collective-permute-start(bf16[16,4096]{1,0:T(8,128)(2,1)S(1)} %fusion), channel_id=1, source_target_pairs={{0,24},{1,25},{2,26},{3,27},{4,28},{5,29},{6,30},{7,31},{8,32},{9,... | collective-permute-start | bytes 393224
  1558.0 65.7 %collective-permute-start.22 = (bf16[16,4096]{1,0:T(8,128)(2,1)S(1)}, bf16[16,4096]{1,0:T(8,128)(2,1)}, u32[]{:S(2)}, u32[]{:S(2)}) collective-permute-start(bf16[16,4096]{1,0:T(8,128)(2,1)S(1)} %fusion), channel_id=1, source_target_pairs={{0,23},{1,24},{2,25},{3,26},{4,27},{5,28},{6,29},{7,30},{8,31},{9,... | collective-permute-start | bytes 393224
  1571.2 65.7 %collective-permute-start.21 = (bf16[16,4096]{1,0:T(8,128)(2,1)S(1)}, bf16[16,4096]{1,0:T(8,128)(2,1)}, u32[]{:S(2)}, u32[]{:S(2)}) collective-permute-start(bf16[16,4096]{1,0:T(8,128)(2,1)S(1)} %fusion), channel_id=1, source_target_pairs={{0,22},{1,23},{2,24},{3,25},{4,26},{5,27},{6,28},{7,29},{8,30},{9,... | collective-permute-start | bytes 393224
  1584.3 65.7 %collective-permute-start.20 = (bf16[16,4096]{1,0:T(8,128)(2,1)S(1)}, bf16[16,4096]{1,0:T(8,128)(2,1)}, u32[]{:S(2)}, u32[]{:S(2)}) collective-permute-start(bf16[16,4096]{1,0:T(8,128)(2,1)S(1)} %fusion), channel_id=1, source_target_pairs={{0,21},{1,22},{2,23},{3,24},{4,25},{5,26},{6,27},{7,28},{8,29},{9,... | collective-permute-start | bytes 393224
  1597.5 65.7 %collective-permute-start.19 = (bf16[16,4096]{1,0:T(8,128)(2,1)S(1)}, bf16[16,4096]{1,0:T(8,128)(2,1)}, u32[]{:S(2)}, u32[]{:S(2)}) collective-permute-start(bf16[16,4096]{1,0:T(8,128)(2,1)S(1)} %fusion), channel_id=1, source_target_pairs={{0,20},{1,21},{2,22},{3,23},{4,24},{5,25},{6,26},{7,27},{8,28},{9,... | collective-permute-start | bytes 393224
  1610.7 65.7 %collective-permute-start.18 = (bf16[16,4096]{1,0:T(8,128)(2,1)S(1)}, bf16[16,4096]{1,0:T(8,128)(2,1)}, u32[]{:S(2)}, u32[]{:S(2)}) collective-permute-start(bf16[16,4096]{1,0:T(8,128)(2,1)S(1)} %fusion), channel_id=1, source_target_pairs={{0,19},{1,20},{2,21},{3,22},{4,23},{5,24},{6,25},{7,26},{8,27},{9,... | collective-permute-start | bytes 393224
  1623.8 65.7 %collective-permute-start.17 = (bf16[16,4096]{1,0:T(8,128)(2,1)S(1)}, bf16[16,4096]{1,0:T(8,128)(2,1)}, u32[]{:S(2)}, u32[]{:S(2)}) collective-permute-start(bf16[16,4096]{1,0:T(8,128)(2,1)S(1)} %fusion), channel_id=1, source_target_pairs={{0,18},{1,19},{2,20},{3,21},{4,22},{5,23},{6,24},{7,25},{8,26},{9,... | collective-permute-start | bytes 393224
  1636.9 65.7 %collective-permute-start.16 = (bf16[16,4096]{1,0:T(8,128)(2,1)S(1)}, bf16[16,4096]{1,0:T(8,128)(2,1)}, u32[]{:S(2)}, u32[]{:S(2)}) collective-permute-start(bf16[16,4096]{1,0:T(8,128)(2,1)S(1)} %fusion), channel_id=1, source_target_pairs={{0,17},{1,18},{2,19},{3,20},{4,21},{5,22},{6,23},{7,24},{8,25},{9,... | collective-permute-start | bytes 393224
  1650.1 65.7 %collective-permute-start.15 = (bf16[16,4096]{1,0:T(8,128)(2,1)S(1)}, bf16[16,4096]{1,0:T(8,128)(2,1)}, u32[]{:S(2)}, u32[]{:S(2)}) collective-permute-start(bf16[16,4096]{1,0:T(8,128)(2,1)S(1)} %fusion), channel_id=1, source_target_pairs={{0,16},{1,17},{2,18},{3,19},{4,20},{5,21},{6,22},{7,23},{8,24},{9,... | collective-permute-start | bytes 393224
  1663.2 67.4 %collective-permute-start.14 = (bf16[16,4096]{1,0:T(8,128)(2,1)S(1)}, bf16[16,4096]{1,0:T(8,128)(2,1)}, u32[]{:S(2)}, u32[]{:S(2)}) collective-permute-start(bf16[16,4096]{1,0:T(8,128)(2,1)S(1)} %fusion), channel_id=1, source_target_pairs={{0,15},{1,16},{2,17},{3,18},{4,19},{5,20},{6,21},{7,22},{8,23},{9,... | collective-permute-start | bytes 393224
  1676.4 67.4 %collective-permute-start.13 = (bf16[16,4096]{1,0:T(8,128)(2,1)S(1)}, bf16[16,4096]{1,0:T(8,128)(2,1)}, u32[]{:S(2)}, u32[]{:S(2)}) collective-permute-start(bf16[16,4096]{1,0:T(8,128)(2,1)S(1)} %fusion), channel_id=1, source_target_pairs={{0,14},{1,15},{2,16},{3,17},{4,18},{5,19},{6,20},{7,21},{8,22},{9,... | collective-permute-start | bytes 393224
  1689.5 67.4 %collective-permute-start.12 = (bf16[16,4096]{1,0:T(8,128)(2,1)S(1)}, bf16[16,4096]{1,0:T(8,128)(2,1)}, u32[]{:S(2)}, u32[]{:S(2)}) collective-permute-start(bf16[16,4096]{1,0:T(8,128)(2,1)S(1)} %fusion), channel_id=1, source_target_pairs={{0,13},{1,14},{2,15},{3,16},{4,17},{5,18},{6,19},{7,20},{8,21},{9,... | collective-permute-start | bytes 393224
  1702.6 67.4 %collective-permute-start.11 = (bf16[16,4096]{1,0:T(8,128)(2,1)S(1)}, bf16[16,4096]{1,0:T(8,128)(2,1)}, u32[]{:S(2)}, u32[]{:S(2)}) collective-permute-start(bf16[16,4096]{1,0:T(8,128)(2,1)S(1)} %fusion), channel_id=1, source_target_pairs={{0,12},{1,13},{2,14},{3,15},{4,16},{5,17},{6,18},{7,19},{8,20},{9,... | collective-permute-start | bytes 393224
  1716.2 67.0 %collective-permute-start.10 = (bf16[16,4096]{1,0:T(8,128)(2,1)S(1)}, bf16[16,4096]{1,0:T(8,128)(2,1)}, u32[]{:S(2)}, u32[]{:S(2)}) collective-permute-start(bf16[16,4096]{1,0:T(8,128)(2,1)S(1)} %fusion), channel_id=1, source_target_pairs={{0,11},{1,12},{2,13},{3,14},{4,15},{5,16},{6,17},{7,18},{8,19},{9,... | collective-permute-start | bytes 393224
  1730.7 68.6 %collective-permute-start.9 = (bf16[16,4096]{1,0:T(8,128)(2,1)S(1)}, bf16[16,4096]{1,0:T(8,128)(2,1)}, u32[]{:S(2)}, u32[]{:S(2)}) collective-permute-start(bf16[16,4096]{1,0:T(8,128)(2,1)S(1)} %fusion), channel_id=1, source_target_pairs={{0,10},{1,11},{2,12},{3,13},{4,14},{5,15},{6,16},{7,17},{8,18},{9,... | collective-permute-start | bytes 393224
  1743.8 68.6 %collective-permute-start.8 = (bf16[16,4096]{1,0:T(8,128)(2,1)S(1)}, bf16[16,4096]{1,0:T(8,128)(2,1)}, u32[]{:S(2)}, u32[]{:S(2)}) collective-permute-start(bf16[16,4096]{1,0:T(8,128)(2,1)S(1)} %fusion), channel_id=1, source_target_pairs={{0,9},{1,10},{2,11},{3,12},{4,13},{5,14},{6,15},{7,16},{8,17},{9,1... | collective-permute-start | bytes 393224
  1756.9 68.6 %collective-permute-start.7 = (bf16[16,4096]{1,0:T(8,128)(2,1)S(1)}, bf16[16,4096]{1,0:T(8,128)(2,1)}, u32[]{:S(2)}, u32[]{:S(2)}) collective-permute-start(bf16[16,4096]{1,0:T(8,128)(2,1)S(1)} %fusion), channel_id=1, source_target_pairs={{0,8},{1,9},{2,10},{3,11},{4,12},{5,13},{6,14},{7,15},{8,16},{9,17... | collective-permute-start | bytes 393224
  1770.1 68.6 %collective-permute-start.6 = (bf16[16,4096]{1,0:T(8,128)(2,1)S(1)}, bf16[16,4096]{1,0:T(8,128)(2,1)}, u32[]{:S(2)}, u32[]{:S(2)}) collective-permute-start(bf16[16,4096]{1,0:T(8,128)(2,1)S(1)} %fusion), channel_id=1, source_target_pairs={{0,7},{1,8},{2,9},{3,10},{4,11},{5,12},{6,13},{7,14},{8,15},{9,16}... | collective-permute-start | bytes 393224
  1783.2 68.6 %collective-permute-start.5 = (bf16[16,4096]{1,0:T(8,128)(2,1)S(1)}, bf16[16,4096]{1,0:T(8,128)(2,1)}, u32[]{:S(2)}, u32[]{:S(2)}) collective-permute-start(bf16[16,4096]{1,0:T(8,128)(2,1)S(1)} %fusion), channel_id=1, source_target_pairs={{0,6},{1,7},{2,8},{3,9},{4,10},{5,11},{6,12},{7,13},{8,14},{9,15},... | collective-permute-start | bytes 393224
  1799.3 66.2 %collective-permute-start.4 = (bf16[16,4096]{1,0:T(8,128)(2,1)S(1)}, bf16[16,4096]{1,0:T(8,128)(2,1)S(1)}, u32[]{:S(2)}, u32[]{:S(2)}) collective-permute-start(bf16[16,4096]{1,0:T(8,128)(2,1)S(1)} %fusion), channel_id=1, source_target_pairs={{0,5},{1,6},{2,7},{3,8},{4,9},{5,10},{6,11},{7,12},{8,13},{9,14},{... | collective-permute-start | bytes 393224
  (78 other events, 12186.5 us)
Sparse Core Ops, SparseCore 0:
  9.9 457.4 all-gather.2
